TPU v7x, 32 devices: a whole 2x2x4 slice. The times are simulated.
32 devices in a mesh: videos: 2 (over y), rows: 4 (over z), cols: 4 (over x, core).
Axes of the slice: x: 2, y: 2, z: 4, core: 2. Of those that a mesh axis runs over, the one named last changes fastest.
Arguments:
- hidden: bfloat16 [2, 16, 128, 384], P('videos', 'rows', 'cols'), parts along dimension 0, may hold values from -40 to 40
- frame_cache: bfloat16 [2, 2, 16, 128, 384], P('videos', None, 'rows', 'cols'), parts along dimension 0, may hold values from -6 to 6
- shortcut: bfloat16 [2, 16, 128, 384], P('videos', 'rows', 'cols'), parts along dimension 0, may hold values from -40 to 40
- gain_one: float32 [384], replicated, may hold values from 0.5 to 1.5
- conv_weight: bfloat16 [3, 3, 3, 384, 384], replicated, may hold values from -0.0625 to 0.0625
- conv_bias: float32 [384], replicated, may hold values from -2 to 2
- gain_two: float32 [384], replicated, may hold values from 0.5 to 1.5
- query_weight: bfloat16 [384, 384], replicated, may hold values from -1 to 1
- query_bias: float32 [384], replicated, may hold values from -3 to 3
- key_weight: bfloat16 [384, 384], replicated, may hold values from -1 to 1
- value_weight: bfloat16 [384, 384], replicated, may hold values from -0.3125 to 0.3125
- value_bias: float32 [384], replicated, may hold values from -3 to 3
- out_weight: bfloat16 [384, 384], replicated, may hold values from -0.3125 to 0.3125
- out_bias: float32 [384], replicated, may hold values from -2 to 2
Outputs:
- decoded: bfloat16 [2, 16, 128, 384], P('videos', 'rows', 'cols'), parts along dimension 0
There are 2 independent parts, one for each index of `videos`. A program takes and returns all parts, laid end to end along the dimension named above; an argument that names none is the same for every part. Nothing has to cross between parts.
All inputs are finite; a program needn't handle non-finite values.
Results may differ from a plain program's by a relative error of at most 0.0065.
Values may be sent and summed in bfloat16 or wider, within the bound.
A program may use at most 128 MiB of HBM per device.

v0:
```python
import jax
import jax.numpy as jnp
from jax import lax
from jax.sharding import PartitionSpec as P

norm_epsilon = 1e-06


def padded(cells, sides, width):
    for axis, dim in sides:
        count = lax.axis_size(axis)
        ends = count - 1
        head = lax.slice_in_dim(cells, 0, width, axis=dim)
        tail = lax.slice_in_dim(cells, cells.shape[dim] - width, cells.shape[dim], axis=dim)
        cells = jnp.concatenate(
            [
                lax.ppermute(tail, axis, [(i, (i + 1) % count) for i in range(ends)]),
                cells,
                lax.ppermute(head, axis, [((i + 1) % count, i) for i in range(ends)]),
            ],
            axis=dim,
        )
    return cells


def normalize(field_rows, gain):
    mean_square = jnp.mean(field_rows * field_rows, axis=1, keepdims=True)
    return field_rows * lax.rsqrt(mean_square + norm_epsilon) * gain


def per_device(
    hidden,
    frame_cache,
    shortcut,
    gain_one,
    conv_weight,
    conv_bias,
    gain_two,
    query_weight,
    query_bias,
    key_weight,
    value_weight,
    value_bias,
    out_weight,
    out_bias,
):
    tile_rows = hidden.shape[1]
    tile_cols = hidden.shape[2]
    channels = hidden.shape[3]
    current = hidden[0].reshape(tile_rows * tile_cols, channels).astype(jnp.float32)
    activated = jax.nn.silu(normalize(current, gain_one)).astype(jnp.bfloat16)
    stacked = jnp.concatenate(
        [frame_cache[0], activated.reshape(1, tile_rows, tile_cols, channels)], axis=0
    )
    rimmed = padded(stacked, (("rows", 1), ("cols", 2)), 1)
    convolved = (
        lax.conv_general_dilated(
            rimmed[None],
            conv_weight,
            (1, 1, 1),
            "VALID",
            dimension_numbers=("NDHWC", "DHWIO", "NDHWC"),
            preferred_element_type=jnp.float32,
        )[0, 0]
        + conv_bias
    )
    mixed = (
        (shortcut[0].astype(jnp.float32) + convolved)
        .astype(jnp.bfloat16)
        .reshape(tile_rows * tile_cols, channels)
    )
    normed = normalize(mixed.astype(jnp.float32), gain_two).astype(jnp.bfloat16)
    queries = (
        jnp.dot(normed, query_weight, preferred_element_type=jnp.float32) + query_bias
    ).astype(jnp.bfloat16)
    score_scale = float(channels) ** (-0.5)
    query_count = queries.shape[0]
    piece = lax.all_gather(normed, ("rows", "cols"), axis=0, tiled=True)
    key_rows = jnp.dot(piece, key_weight, preferred_element_type=jnp.float32).astype(jnp.bfloat16)
    value_rows = (
        jnp.dot(piece, value_weight, preferred_element_type=jnp.float32) + value_bias
    ).astype(jnp.bfloat16)
    running_max = jnp.full((query_count,), -1e30, jnp.float32)
    scores = (
        jnp.einsum("qc,kc->qk", queries, key_rows, preferred_element_type=jnp.float32) * score_scale
    )
    new_max = jnp.maximum(running_max, jnp.max(scores, axis=1))
    expos = jnp.exp(scores - new_max[:, None])
    new_sum = jnp.sum(expos, axis=1)
    new_weighted = jnp.dot(
        expos.astype(jnp.bfloat16), value_rows, preferred_element_type=jnp.float32
    )
    attended = (new_weighted / new_sum[:, None]).astype(jnp.bfloat16)
    projected = jnp.dot(attended, out_weight, preferred_element_type=jnp.float32) + out_bias
    decoded = (mixed.astype(jnp.float32) + projected).astype(jnp.bfloat16)
    return decoded.reshape(1, tile_rows, tile_cols, channels)


def solution(mesh):
    placed = (
        P("videos", "rows", "cols", None),
        P("videos", None, "rows", "cols", None),
        P("videos", "rows", "cols", None),
        P(),
        P(),
        P(),
        P(),
        P(),
        P(),
        P(),
        P(),
        P(),
        P(),
        P(),
    )
    return jax.shard_map(
        per_device,
        mesh=mesh,
        in_specs=placed,
        out_specs=P("videos", "rows", "cols", None),
        check_vma=False,
    )
```

profile of v0, /device:TPU:0, one launch (start us, length us, event | category | flops | bytes accessed | tf_op | source)
XLA Modules:
  0.0 91.4 jit_solution(13943314025765096930)
XLA Ops:
  6.5 1.0 %fusion.18 = f32[4,32]{1,0:T(4,128)S(1)} fusion(bf16[1,4,32,384]{3,2,1,0:T(8,128)(2,1)} %param.14), kind=kLoop, calls=%fused_computation.28 | loop fusion | flops 147328 | bytes 98816 | tf_op jit(solution)/shard_map/reduce_sum | solution.py:27
  7.6 1.0 %fusion.25 = bf16[1,4,32,384]{3,2,1,0:T(8,128)(2,1)S(1)} fusion(bf16[1,4,32,384]{3,2,1,0:T(8,128)(2,1)} %param.14, f32[384]{0:T(512)} %param.17, f32[4,32]{1,0:T(4,128)S(1)} %add_rsqrt_fusion.1), kind=kLoop, calls=%fused_computation.35 | loop fusion | flops 393216 | bytes 198656 | tf_op jit(solution)/shard_map/convert_element_type | solution.py:51
  8.6 0.9 pad_maximum_fusion.1
  9.5 4.9 %collective-permute-start = (bf16[3,1,32,384]{3,2,1,0:T(8,128)(2,1)S(1)}, bf16[3,1,32,384]{3,2,1,0:T(8,128)(2,1)S(1)}, u32[]{:S(2)}, u32[]{:S(2)}) collective-permute-start(bf16[3,1,32,384]{3,2,1,0:T(8,128)(2,1)S(1)} %get-tuple-element.9), channel_id=1, source_target_pairs={{0,4},{4,8},{8,12},{1,5},{5,9},{9,13},{2,6},{6,10},{10,14},{3,7},{... | collective-permute-start | bytes 221192 | tf_op jit(solution)/shard_map/ppermute | solution.py:17
  14.4 1.3 %collective-permute-start.1 = (bf16[3,1,32,384]{3,2,1,0:T(8,128)(2,1)S(1)}, bf16[3,1,32,384]{3,2,1,0:T(8,128)(2,1)S(1)}, u32[]{:S(2)}, u32[]{:S(2)}) collective-permute-start(bf16[3,1,32,384]{3,2,1,0:T(8,128)(2,1)S(1)} %get-tuple-element.10), channel_id=1, source_target_pairs={{4,0},{8,4},{12,8},{5,1},{9,5},{13,9},{6,2},{10,6},{14,10},{7,3},{... | collective-permute-start | bytes 221192 | tf_op jit(solution)/shard_map/ppermute | solution.py:19
  15.7 0.7 collective-permute-done
  16.4 4.3 %collective-permute-done.1 = bf16[3,1,32,384]{3,2,1,0:T(8,128)(2,1)S(1)} collective-permute-done((bf16[3,1,32,384]{3,2,1,0:T(8,128)(2,1)S(1)}, bf16[3,1,32,384]{3,2,1,0:T(8,128)(2,1)S(1)}, u32[]{:S(2)}, u32[]{:S(2)}) %collective-permute-start.1) | collective-permute-done | bytes 73760 | tf_op jit(solution)/shard_map/ppermute | solution.py:19
  20.7 0.9 pad_maximum_fusion.5
  21.5 1.3 %collective-permute-start.2 = (bf16[3,6,1,384]{3,2,1,0:T(2,128)(2,1)S(1)}, bf16[3,6,1,384]{3,2,1,0:T(2,128)(2,1)S(1)}, u32[]{:S(2)}, u32[]{:S(2)}) collective-permute-start(bf16[3,6,1,384]{3,2,1,0:T(2,128)(2,1)S(1)} %get-tuple-element.7), channel_id=1, source_target_pairs={{0,1},{1,2},{2,3},{4,5},{5,6},{6,7},{8,9},{9,10},{10,11},{12,13},{... | collective-permute-start | bytes 41480 | tf_op jit(solution)/shard_map/ppermute | solution.py:17
  22.8 1.3 %collective-permute-start.3 = (bf16[3,6,1,384]{3,2,1,0:T(2,128)(2,1)S(1)}, bf16[3,6,1,384]{3,2,1,0:T(2,128)(2,1)S(1)}, u32[]{:S(2)}, u32[]{:S(2)}) collective-permute-start(bf16[3,6,1,384]{3,2,1,0:T(2,128)(2,1)S(1)} %get-tuple-element.8), channel_id=1, source_target_pairs={{1,0},{2,1},{3,2},{5,4},{6,5},{7,6},{9,8},{10,9},{11,10},{13,12},{... | collective-permute-start | bytes 41480 | tf_op jit(solution)/shard_map/ppermute | solution.py:19
  24.1 3.5 %collective-permute-done.3 = bf16[3,6,1,384]{3,2,1,0:T(2,128)(2,1)S(1)} collective-permute-done((bf16[3,6,1,384]{3,2,1,0:T(2,128)(2,1)S(1)}, bf16[3,6,1,384]{3,2,1,0:T(2,128)(2,1)S(1)}, u32[]{:S(2)}, u32[]{:S(2)}) %collective-permute-start.3) | collective-permute-done | bytes 13856 | tf_op jit(solution)/shard_map/ppermute | solution.py:19
  27.7 1.2 %maximum_bitcast_fusion = bf16[3,6,1,34,384]{4,3,1,0,2:T(8,128)(2,1)S(1)} fusion(bf16[3,6,1,384]{3,2,1,0:T(2,128)(2,1)S(1)} %collective-permute-done.3, bf16[3,1,32,384]{3,2,1,0:T(8,128)(2,1)S(1)} %collective-permute-done.1, bf16[1,4,32,384]{3,2,1,0:T(8,128)(2,1)S(1)} %fusion.25, bf16[2,4,32,384]{3,2,1,0:T(8,128)(2,1)} %bitcast.40, ...), kind=kLoop, calls=%fused_computation.22 | loop fusion | flops 2820096 | bytes 940032 | tf_op jit(solution)/shard_map/broadcast_in_dim | solution.py:58
  29.0 0.1 pad.clone
  29.2 0.4 copy-done.10
  29.6 5.2 %convolution_select_fusion = f32[1,4,8,5,384]{4,2,3,1,0:T(8,128)S(1)} fusion(bf16[3,3,3,384,384]{4,3,2,1,0:T(8,128)(2,1)} %param.18, bf16[3,6,1,7,2,384]{5,3,4,1,0,2:T(8,128)(2,1)S(1)} %slice.18, bf16[3,6,1,8,5,384]{5,3,4,1,0,2:T(8,128)(2,1)S(1)} %copy.41, pred[8,5]{0,1:T(8,128)(4,1)S(1)} %copy-done.10), kind=kOutput, calls=%fused_computation.9 | convolution fusion | flops 1276403712 | bytes 8954920 | tf_op jit(solution)/shard_map/conv_general_dilated | solution.py:57
  35.0 0.1 multiply_reduce_fusion
  35.2 0.3 copy-done.5
  35.5 0.7 fusion.27
  36.3 1.1 %fusion.3 = bf16[128,384]{1,0:T(8,128)(2,1)S(1)} fusion(bf16[128,384]{1,0:T(8,128)(2,1)} %get-tuple-element.5, bf16[384,384]{1,0:T(8,128)(2,1)S(1)} %copy-done.3, f32[384]{0:T(512)S(1)} %copy-done.6), kind=kOutput, calls=%fused_computation.10 | convolution fusion | flops 37847040 | bytes 493056 | tf_op jit(solution)/shard_map/dot_general | solution.py:74
  37.4 40.2 %all-gather.2.cloned.1.call-done = bf16[2048,384]{1,0:T(8,128)(2,1)} async-done(((bf16[128,384]{1,0:T(8,128)(2,1)}), bf16[2048,384]{1,0:T(8,128)(2,1)}) %all-gather.2.cloned.1.call-update) | async-done | bytes 1572880 | tf_op jit(solution)/shard_map/all_gather | solution.py:78
  77.7 3.1 %fusion.36 = (f32[128]{0:T(128)S(1)}, f32[128,2048]{1,0:T(8,128)S(1)}) fusion(bf16[128,384]{1,0:T(8,128)(2,1)S(1)} %fusion.3, bf16[2048,384]{1,0:T(8,128)(2,1)} %all-gather.2.cloned.1.call-done, bf16[384,384]{1,0:T(8,128)(2,1)S(1)} %copy-done), kind=kOutput, calls=%fused_computation.57 | convolution fusion | flops 806616960 | bytes 3015168 | tf_op jit(solution)/shard_map/qc,kc->qk/dot_general | solution.py:85
  80.8 0.3 fusion.7
  81.1 2.6 %fusion.6 = bf16[128,384]{1,0:T(8,128)(2,1)S(1)} fusion(bf16[2048,384]{1,0:T(8,128)(2,1)S(1)} %copy-done.8, bf16[384,384]{1,0:T(8,128)(2,1)} %param.24, f32[384]{0:T(512)S(1)} %copy-done.9, f32[128,2048]{1,0:T(8,128)S(1)} %get-tuple-element.12, f32[128]{0:T(128)S(1)} %broadcast_maximum_fusion, f32[128]{0:T(128)S(1)} %fusion.7), kind=kOutput, calls=%fused_computation.13 | convolution fusion | flops 807501824 | bytes 3017216 | tf_op jit(solution)/shard_map/dot_general | solution.py:90
  83.7 0.9 fusion.4
  (33 shorter events, 0.5 us)
Async XLA Ops:
  6.5 71.1 %copy-start = (bf16[384,384]{1,0:T(8,128)(2,1)S(1)}, bf16[384,384]{1,0:T(8,128)(2,1)}, u32[]{:S(2)}) copy-start(bf16[384,384]{1,0:T(8,128)(2,1)} %param.23) | copy-start | bytes 884740
  6.5 71.1 %all-gather.2.cloned.1.call-start = ((), (), s32[]{:S(2)}) async-start(), calls=%async_computation | async-start | bytes 1671168 | tf_op jit(solution)/shard_map/all_gather | solution.py:78
  9.5 6.9 %collective-permute-start = (bf16[3,1,32,384]{3,2,1,0:T(8,128)(2,1)S(1)}, bf16[3,1,32,384]{3,2,1,0:T(8,128)(2,1)S(1)}, u32[]{:S(2)}, u32[]{:S(2)}) collective-permute-start(bf16[3,1,32,384]{3,2,1,0:T(8,128)(2,1)S(1)} %get-tuple-element.9), channel_id=1, source_target_pairs={{0,4},{4,8},{8,12},{1,5},{5,9},{9,13},{2,6},{6,10},{10,14},{3,7},{... | collective-permute-start | bytes 221192 | tf_op jit(solution)/shard_map/ppermute | solution.py:17
  14.4 6.2 %collective-permute-start.1 = (bf16[3,1,32,384]{3,2,1,0:T(8,128)(2,1)S(1)}, bf16[3,1,32,384]{3,2,1,0:T(8,128)(2,1)S(1)}, u32[]{:S(2)}, u32[]{:S(2)}) collective-permute-start(bf16[3,1,32,384]{3,2,1,0:T(8,128)(2,1)S(1)} %get-tuple-element.10), channel_id=1, source_target_pairs={{4,0},{8,4},{12,8},{5,1},{9,5},{13,9},{6,2},{10,6},{14,10},{7,3},{... | collective-permute-start | bytes 221192 | tf_op jit(solution)/shard_map/ppermute | solution.py:19
  21.5 2.6 %collective-permute-start.2 = (bf16[3,6,1,384]{3,2,1,0:T(2,128)(2,1)S(1)}, bf16[3,6,1,384]{3,2,1,0:T(2,128)(2,1)S(1)}, u32[]{:S(2)}, u32[]{:S(2)}) collective-permute-start(bf16[3,6,1,384]{3,2,1,0:T(2,128)(2,1)S(1)} %get-tuple-element.7), channel_id=1, source_target_pairs={{0,1},{1,2},{2,3},{4,5},{5,6},{6,7},{8,9},{9,10},{10,11},{12,13},{... | collective-permute-start | bytes 41480 | tf_op jit(solution)/shard_map/ppermute | solution.py:17
  22.8 4.8 %collective-permute-start.3 = (bf16[3,6,1,384]{3,2,1,0:T(2,128)(2,1)S(1)}, bf16[3,6,1,384]{3,2,1,0:T(2,128)(2,1)S(1)}, u32[]{:S(2)}, u32[]{:S(2)}) collective-permute-start(bf16[3,6,1,384]{3,2,1,0:T(2,128)(2,1)S(1)} %get-tuple-element.8), channel_id=1, source_target_pairs={{1,0},{2,1},{3,2},{5,4},{6,5},{7,6},{9,8},{10,9},{11,10},{13,12},{... | collective-permute-start | bytes 41480 | tf_op jit(solution)/shard_map/ppermute | solution.py:19
  28.9 0.7 copy-start.10
  29.6 5.4 %copy-start.1 = (bf16[1,4,32,384]{3,2,1,0:T(8,128)(2,1)S(1)}, bf16[1,4,32,384]{3,2,1,0:T(8,128)(2,1)}, u32[]{:S(2)}) copy-start(bf16[1,4,32,384]{3,2,1,0:T(8,128)(2,1)} %param.16) | copy-start | bytes 294916
  29.6 5.4 %copy-start.4 = (f32[384]{0:T(512)S(1)}, f32[384]{0:T(512)}, u32[]{:S(2)}) copy-start(f32[384]{0:T(512)} %param.19) | copy-start | bytes 4612
  34.8 0.7 copy-start.5
  34.9 1.4 %copy-start.3 = (bf16[384,384]{1,0:T(8,128)(2,1)S(1)}, bf16[384,384]{1,0:T(8,128)(2,1)}, u32[]{:S(2)}) copy-start(bf16[384,384]{1,0:T(8,128)(2,1)} %param.21) | copy-start | bytes 884740
  34.9 1.4 %copy-start.6 = (f32[384]{0:T(512)S(1)}, f32[384]{0:T(512)}, u32[]{:S(2)}) copy-start(f32[384]{0:T(512)} %param.22) | copy-start | bytes 4612
  37.4 43.7 %copy-start.9 = (f32[384]{0:T(512)S(1)}, f32[384]{0:T(512)}, u32[]{:S(2)}) copy-start(f32[384]{0:T(512)} %param.25) | copy-start | bytes 4612
  77.7 3.4 %copy-start.8 = (bf16[2048,384]{1,0:T(8,128)(2,1)S(1)}, bf16[2048,384]{1,0:T(8,128)(2,1)}, u32[]{:S(2)}) copy-start(bf16[2048,384]{1,0:T(8,128)(2,1)} %all-gather.2.cloned.1.call-done) | copy-start | bytes 4718596
  81.1 2.6 %copy-start.2 = (bf16[384,384]{1,0:T(8,128)(2,1)S(1)}, bf16[384,384]{1,0:T(8,128)(2,1)}, u32[]{:S(2)}) copy-start(bf16[384,384]{1,0:T(8,128)(2,1)} %param.26) | copy-start | bytes 884740
  81.1 2.6 %copy-start.7 = (f32[384]{0:T(512)S(1)}, f32[384]{0:T(512)}, u32[]{:S(2)}) copy-start(f32[384]{0:T(512)} %param.27) | copy-start | bytes 4612
Sparse Core Ops, SparseCore 0:
  36.4 41.1 all-gather.1
where the time goes:
time: 91.9 us; the launch traced here: 91.4 us
  waiting for transfers between devices  48.7 us (53%)
  between operations  13.7 us (15%)
  matrix products  12.8 us (14%)
  starting transfers between devices  8.81 us (10%)
  other arithmetic  6.13 us (7%)
  local copies, waits for them, and re-layouts  1.27 us (1%)
    all_gather x1, waiting for transfers between devices, per_device(): piece = lax.all_gather(normed, ('rows', 'cols'), axis=0, tiled=True)  40.2 us
    ppermute x2, waiting for transfers between devices, padded(): lax.ppermute(head, axis, [((i + 1) % count, i) for i in range(ends)])  7.79 us
    ppermute x2, starting transfers between devices, padded(): lax.ppermute(tail, axis, [(i, (i + 1) % count) for i in range(ends)])  6.22 us
    conv_general_dilated x1, matrix products, per_device(): lax.conv_general_dilated(rimmed[None], conv_weight, (1, 1, 1), 'VALID', d...  5.21 us
    dot_general x1, matrix products, per_device(): jnp.einsum('qc,kc->qk', queries, key_rows, preferred_element_type=jnp.flo...  3.12 us
    ppermute x2, starting transfers between devices, padded(): lax.ppermute(head, axis, [((i + 1) % count, i) for i in range(ends)])  2.58 us
    dot_general x1, matrix products, per_device(): jnp.dot(expos.astype(jnp.bfloat16), value_rows, preferred_element_type=jn...  2.56 us
  transfers between devices with their start and end apart: 5, of which 4 were waited for; matrix products, arithmetic and copies ran while one was open for 1% of the time, Pallas kernels for 0%

commit v1 on v0

v1 whole, which is shorter than its diff:
```python
import functools
import math

import jax
import jax.numpy as jnp
from jax import lax
from jax.experimental import pallas as pl
from jax.experimental.pallas import tpu as pltpu
from jax.sharding import PartitionSpec as P

norm_epsilon = 1e-06
f32 = jnp.float32
bf16 = jnp.bfloat16
MESH = pl.DeviceIdType.MESH


def normalize(field_rows, gain):
    mean_square = jnp.mean(field_rows * field_rows, axis=1, keepdims=True)
    return field_rows * lax.rsqrt(mean_square + norm_epsilon) * gain


def kernel(
    R, K, cores, TR, TC, C, E,
    hidden_ref, cache_ref, shortcut_ref, gain_one_ref, conv_bias_ref, gain_two_ref,
    query_bias_ref, value_bias_ref, out_bias_ref,
    conv_hbm, query_hbm, key_hbm, value_hbm, out_hbm,
    o_ref,
    conv_w, proj_w, xs, sr, sc, hr, hc, edge, G, run_max, run_sum, acc,
    conv_sem, proj_sem, hsend, hrecv, zsem, xsem, csem, rsem,
):
    X = K // cores
    N = TR * TC
    r = lax.axis_index("rows")
    col = lax.axis_index("cols")
    x = col // cores
    c = col % cores

    has_up = r > 0
    has_down = r < R - 1
    rows_ok = (has_up, None, has_down)

    def exists(dr, dc):
        ok = None
        if dr:
            ok = rows_ok[dr + 1]
        if dc:
            side = (col > 0) if dc < 0 else (col < K - 1)
            ok = side if ok is None else jnp.logical_and(ok, side)
        return ok

    neighbours = [(-1, 0), (1, 0)] + [(dr, dc) for dc in (-1, 1) for dr in (-1, 0, 1)]
    barrier = pltpu.get_barrier_semaphore()
    expected = jnp.int32(X - 1)
    for dr, dc in neighbours:
        ok = exists(dr, dc)

        @pl.when(ok)
        def _():
            pl.semaphore_signal(
                barrier, inc=1, device_id={"rows": r + dr, "cols": col + dc}, device_id_type=MESH
            )

        expected = expected + ok.astype(jnp.int32)
    x_peers = [lax.rem(x + d, X) for d in range(1, X)]
    for xp in x_peers:
        pl.semaphore_signal(
            barrier, inc=1, device_id={"rows": r, "cols": xp * cores + c}, device_id_type=MESH
        )

    conv_copies = [
        pltpu.make_async_copy(conv_hbm.at[k], conv_w.at[k], conv_sem.at[k]) for k in range(9)
    ]
    proj_copies = [
        pltpu.make_async_copy(source, proj_w.at[k], proj_sem.at[k])
        for k, source in enumerate((query_hbm, key_hbm, value_hbm, out_hbm))
    ]
    for copy in conv_copies + proj_copies:
        copy.start()

    current = normalize(hidden_ref[...].astype(f32), gain_one_ref[...])
    activated = (current / (1.0 + jnp.exp(-current))).astype(bf16)
    position = lax.broadcasted_iota(jnp.int32, (16, 1), 0)
    for f in range(3):
        frame = activated if f == 2 else cache_ref[f]
        sr[0, f * TC : (f + 1) * TC] = frame[:TC]
        sr[1, f * TC : (f + 1) * TC] = frame[N - TC :]
        wide = frame.astype(f32)
        for i in range(TR):
            k = f * TR + i
            edge[0, k : k + 1] = wide[i * TC : i * TC + 1]
            edge[1, k : k + 1] = wide[(i + 1) * TC - 1 : (i + 1) * TC]
        xs[f, TC : TC + N, C : 2 * C] = frame
        xs[f, TC : TC + N, 0:C] = pltpu.roll(wide, 1, 0).astype(bf16)
        xs[f, TC : TC + N, 2 * C : 3 * C] = pltpu.roll(wide, N - 1, 0).astype(bf16)
    if E > 3 * TR:
        for side in range(2):
            edge[side, 3 * TR : E] = jnp.zeros((E - 3 * TR, C), f32)
    sc[...] = edge[...].astype(bf16)

    pl.semaphore_wait(barrier, expected)

    def halo(dr, dc):
        if dc == 0:
            slot = 1 if dr < 0 else 0
            source, target = sr.at[0 if dr < 0 else 1], hr.at[slot]
        else:
            side = 1 if dc < 0 else 0
            v = 1 - dr
            slot = 2 + side * 3 + v
            source, target = sc.at[0 if dc < 0 else 1], hc.at[side, v]
        return pltpu.make_async_remote_copy(
            src_ref=source, dst_ref=target, send_sem=hsend.at[slot], recv_sem=hrecv.at[slot],
            device_id={"rows": r + dr, "cols": col + dc}, device_id_type=MESH,
        )

    for dr, dc in neighbours:

        @pl.when(exists(dr, dc))
        def _():
            halo(dr, dc).start()

    for dr, dc in neighbours:
        ok = exists(dr, dc)

        @pl.when(ok)
        def _():
            halo(-dr, -dc).wait_recv()

        @pl.when(jnp.logical_not(ok))
        def _():
            if dc == 0:
                hr[0 if dr < 0 else 1] = jnp.zeros((3 * TC, C), bf16)
            else:
                hc[0 if dc < 0 else 1, dr + 1] = jnp.zeros((E, C), bf16)

    sides = [[hc[side, v].astype(f32) for v in range(3)] for side in range(2)]
    for f in range(3):
        for slot, start in ((0, 0), (1, TC + N)):
            line = hr[slot, f * TC : (f + 1) * TC]
            wide = line.astype(f32)
            xs[f, start : start + TC, C : 2 * C] = line
            xs[f, start : start + TC, 0:C] = pltpu.roll(wide, 1, 0).astype(bf16)
            xs[f, start : start + TC, 2 * C : 3 * C] = pltpu.roll(wide, TC - 1, 0).astype(bf16)
        for i in range(TR + 2):
            if i == 0:
                v, k = 0, f * TR + TR - 1
            elif i == TR + 1:
                v, k = 2, f * TR
            else:
                v, k = 1, f * TR + i - 1
            first = slice(i * TC, i * TC + 16)
            last = slice((i + 1) * TC - 16, (i + 1) * TC)
            xs[f, first, 0:C] = jnp.where(
                position == 0, sides[0][v][k : k + 1], xs[f, first, 0:C].astype(f32)
            ).astype(bf16)
            xs[f, last, 2 * C : 3 * C] = jnp.where(
                position == 15, sides[1][v][k : k + 1], xs[f, last, 2 * C : 3 * C].astype(f32)
            ).astype(bf16)

    total = jnp.zeros((N, C), f32)
    for f in range(3):
        for a in range(3):
            conv_copies[f * 3 + a].wait()
            total = total + jnp.dot(
                xs[f, a * TC : a * TC + N], conv_w[f * 3 + a], preferred_element_type=f32
            )
    mixed = (shortcut_ref[...].astype(f32) + (total + conv_bias_ref[...])).astype(bf16)
    o_ref[...] = mixed
    normed = normalize(mixed.astype(f32), gain_two_ref[...]).astype(bf16)

    def span(which):
        return pl.ds(pl.multiple_of(which * N, N), N)

    G[r, span(col)] = normed

    def move(origin, which, send, row_to, col_to):
        block = G.at[origin, span(which)]
        return pltpu.make_async_remote_copy(
            src_ref=block, dst_ref=block, send_sem=send, recv_sem=rsem.at[origin, which],
            device_id={"rows": row_to, "cols": col_to}, device_id_type=MESH,
        )

    def z_move(origin, way):
        return move(origin, col, zsem.at[origin, way], r + (1 if way else -1), col)

    def x_move(origin, d):
        return move(origin, col, xsem.at[origin, d], r, x_peers[d] * cores + c)

    def core_move(origin, xp):
        return move(origin, xp * cores + c, csem.at[origin, xp], r, x * cores + 1 - c)

    def z_conditions(origin):
        return (
            jnp.logical_and(origin >= r, has_up),
            jnp.logical_and(origin <= r, has_down),
        )

    def spread(origin):
        for way, ok in enumerate(z_conditions(origin)):

            @pl.when(ok)
            def _():
                z_move(origin, way).start()

        for d in range(X - 1):
            x_move(origin, d).start()
        if cores == 2:
            core_move(origin, x).start()

    def arrived(origin, which):
        move(origin, which, zsem.at[origin, 0], r, col).wait_recv()

    def relay(origin):
        for xp in x_peers:
            arrived(origin, xp * cores + c)
            if cores == 2:
                core_move(origin, xp).start()

    def at_distance(s, action):
        @pl.when(r - s >= 0)
        def _():
            action(r - s)

        @pl.when(jnp.logical_and(s > 0, r + s < R))
        def _():
            action(r + s)

    spread(r)

    for copy in proj_copies:
        copy.wait()
    queries = (
        jnp.dot(normed, proj_w[0], preferred_element_type=f32) + query_bias_ref[...]
    ).astype(bf16)
    score_scale = float(C) ** (-0.5) * math.log2(math.e)
    contract_last = (((1,), (1,)), ((), ()))
    folded = (
        lax.dot_general(queries, proj_w[1], contract_last, preferred_element_type=f32)
        * score_scale
    ).astype(bf16)
    run_max[...] = jnp.full((N, 1), -1e30, f32)
    run_sum[...] = jnp.zeros((N, 1), f32)
    acc[...] = jnp.zeros((N, C), f32)

    def attend(origin):
        if cores == 2:
            for xp in range(X):
                arrived(origin, xp * cores + 1 - c)
        piece = G[origin]
        scores = lax.dot_general(folded, piece, contract_last, preferred_element_type=f32)
        old_max = run_max[...]
        new_max = jnp.maximum(old_max, jnp.max(scores, axis=1, keepdims=True))
        keep = jnp.exp2(old_max - new_max)
        expos = jnp.exp2(scores - new_max)
        run_max[...] = new_max
        run_sum[...] = run_sum[...] * keep + jnp.sum(expos, axis=1, keepdims=True)
        acc[...] = acc[...] * keep + jnp.dot(
            expos.astype(bf16), piece, preferred_element_type=f32
        )

    def step(s, carry):
        def receive(origin):
            arrived(origin, col)
            spread(origin)

        at_distance(s, receive)
        at_distance(s - 1, relay)
        return carry

    lax.fori_loop(1, R, step, 0)
    at_distance(R - 1, relay)

    def attend_step(s, carry):
        at_distance(s, attend)
        return carry

    lax.fori_loop(0, R, attend_step, 0)

    context = (acc[...] / run_sum[...]).astype(bf16)
    attended = (
        jnp.dot(context, proj_w[2], preferred_element_type=f32) + value_bias_ref[...]
    ).astype(bf16)
    projected = jnp.dot(attended, proj_w[3], preferred_element_type=f32) + out_bias_ref[...]
    o_ref[...] = (o_ref[...].astype(f32) + projected).astype(bf16)

    for dr, dc in neighbours:

        @pl.when(exists(dr, dc))
        def _():
            halo(dr, dc).wait_send()

    def drain(origin, carry):
        for way, ok in enumerate(z_conditions(origin)):

            @pl.when(ok)
            def _():
                z_move(origin, way).wait_send()

        for d in range(X - 1):
            x_move(origin, d).wait_send()
        if cores == 2:
            for xp in range(X):
                core_move(origin, xp).wait_send()
        return carry

    lax.fori_loop(0, R, drain, 0)


def per_device(
    hidden,
    frame_cache,
    shortcut,
    gain_one,
    conv_weight,
    conv_bias,
    gain_two,
    query_weight,
    query_bias,
    key_weight,
    value_weight,
    value_bias,
    out_weight,
    out_bias,
):
    _, TR, TC, C = hidden.shape
    N = TR * TC
    R = lax.axis_size("rows")
    K = lax.axis_size("cols")
    cores = 2 if K % 2 == 0 else 1
    X = K // cores
    E = -(-3 * TR // 16) * 16
    vector = lambda v: v.reshape(1, C)
    vmem = pl.BlockSpec(memory_space=pltpu.VMEM)
    hbm = pl.BlockSpec(memory_space=pltpu.HBM)
    dma = pltpu.SemaphoreType.DMA
    flops = 2 * N * C * (27 * C + 5 * C + 2 * R * K * N)
    decoded = pl.pallas_call(
        functools.partial(kernel, R, K, cores, TR, TC, C, E),
        out_shape=jax.ShapeDtypeStruct((N, C), bf16),
        in_specs=[vmem] * 9 + [hbm] * 5,
        out_specs=vmem,
        scratch_shapes=[
            pltpu.VMEM((9, 3 * C, C), bf16),
            pltpu.VMEM((4, C, C), bf16),
            pltpu.VMEM((3, N + 2 * TC, 3 * C), bf16),
            pltpu.VMEM((2, 3 * TC, C), bf16),
            pltpu.VMEM((2, E, C), bf16),
            pltpu.VMEM((2, 3 * TC, C), bf16),
            pltpu.VMEM((2, 3, E, C), bf16),
            pltpu.VMEM((2, E, C), f32),
            pltpu.VMEM((R, K * N, C), bf16),
            pltpu.VMEM((N, 1), f32),
            pltpu.VMEM((N, 1), f32),
            pltpu.VMEM((N, C), f32),
            dma((9,)),
            dma((4,)),
            dma((8,)),
            dma((8,)),
            dma((R, 2)),
            dma((R, max(X - 1, 1))),
            dma((R, X)),
            dma((R, K)),
        ],
        compiler_params=pltpu.CompilerParams(
            collective_id=0, has_side_effects=True, vmem_limit_bytes=48 * 1024 * 1024
        ),
        cost_estimate=pl.CostEstimate(
            flops=flops, bytes_accessed=2 * C * (32 * C + 6 * N), transcendentals=R * K * N * N
        ),
    )(
        hidden.reshape(N, C),
        frame_cache.reshape(2, N, C),
        shortcut.reshape(N, C),
        vector(gain_one),
        vector(conv_bias),
        vector(gain_two),
        vector(query_bias),
        vector(value_bias),
        vector(out_bias),
        conv_weight.reshape(9, 3 * C, C),
        query_weight,
        key_weight,
        value_weight,
        out_weight,
    )
    return decoded.reshape(1, TR, TC, C)


def solution(mesh):
    placed = (
        P("videos", "rows", "cols", None),
        P("videos", None, "rows", "cols", None),
        P("videos", "rows", "cols", None),
        P(),
        P(),
        P(),
        P(),
        P(),
        P(),
        P(),
        P(),
        P(),
        P(),
        P(),
    )
    return jax.shard_map(
        per_device,
        mesh=mesh,
        in_specs=placed,
        out_specs=P("videos", "rows", "cols", None),
        check_vma=False,
    )
```

time: 91.9 us -> 41.9 us (0.46)
  waiting for transfers between devices: 48.7 us -> 0 us
  Pallas kernels: 0 us -> 30.1 us
  between operations: 13.7 us -> 0.02 us
  matrix products: 12.8 us -> 0 us
  local copies, waits for them, and re-layouts: 1.27 us -> 11.3 us
  starting transfers between devices: 8.81 us -> 0 us
  other arithmetic: 6.13 us -> 0 us
    all_gather x1 -> x0, waiting for transfers between devices: 40.2 us -> none  [per_device(): piece = lax.all_gather(normed, ('rows', 'cols'), axis=0, tiled=True)]
    pallas_call x0 -> x1, Pallas kernels: none -> 30.1 us  [per_device(): pl.pallas_call(functools.partial(kernel, R, K, cores, TR, TC, C, E), out_...]
    ppermute x4 -> x0, starting transfers between devices: 8.81 us -> none  [the longest x2 6.22 us: padded(): lax.ppermute(tail, axis, [(i, (i + 1) % count) for i in range(ends)])]
    ppermute x4 -> x0, waiting for transfers between devices: 8.46 us -> none  [the longest x2 7.79 us: padded(): lax.ppermute(head, axis, [((i + 1) % count, i) for i in range(ends)])]
    dot_general x4 -> x0, matrix products: 7.64 us -> none  [the longest x1 3.12 us: per_device(): jnp.einsum('qc,kc->qk', queries, key_rows, preferred_element_type=jnp.flo...]
    unnamed x24 -> x15, local copies, waits for them, and re-layouts: 0.86 us -> 7.2 us
    conv_general_dilated x1 -> x0, matrix products: 5.21 us -> none  [per_device(): lax.conv_general_dilated(rimmed[None], conv_weight, (1, 1, 1), 'VALID', d...]
    reshape x0 -> x6, local copies, waits for them, and re-layouts: none -> 4.1 us  [per_device(): vector = lambda v: v.reshape(1, C)]
  transfers between devices with their start and end apart: 5 -> 0, of which waited for: 4 -> 0; matrix products, arithmetic and copies ran while one was open for 1% -> 0% of each run, Pallas kernels for 0% -> 0%
where the time goes in v1:
time: 41.9 us; the launch traced here: 41.4 us
  Pallas kernels  30.1 us (72%)
  local copies, waits for them, and re-layouts  11.3 us (27%)
    pallas_call x1, Pallas kernels, per_device(): pl.pallas_call(functools.partial(kernel, R, K, cores, TR, TC, C, E), out_...  30.1 us
    unnamed x15, local copies, waits for them, and re-layouts  7.2 us
    reshape x6, local copies, waits for them, and re-layouts, per_device(): vector = lambda v: v.reshape(1, C)  4.1 us

profile of v1, /device:TPU:0, one launch (start us, length us, event | category | flops | bytes accessed | tf_op | source)
XLA Modules:
  0.0 41.4 jit_solution(7214431657821600258)
XLA Ops:
  0.0 0.7 %reshape.36.gain_one_ref = f32[1,384]{1,0:T(1,128)S(1)} reshape(f32[384]{0:T(512)} %param.17) | data formatting | bytes 3072 | tf_op jit(solution)/shard_map/reshape | solution.py:332
  0.7 0.7 %reshape.37.conv_bias_ref = f32[1,384]{1,0:T(1,128)S(1)} reshape(f32[384]{0:T(512)} %param.19) | data formatting | bytes 3072 | tf_op jit(solution)/shard_map/reshape | solution.py:332
  1.4 0.7 %reshape.38.gain_two_ref = f32[1,384]{1,0:T(1,128)S(1)} reshape(f32[384]{0:T(512)} %param.20) | data formatting | bytes 3072 | tf_op jit(solution)/shard_map/reshape | solution.py:332
  2.0 0.7 %reshape.39.query_bias_ref = f32[1,384]{1,0:T(1,128)S(1)} reshape(f32[384]{0:T(512)} %param.22) | data formatting | bytes 3072 | tf_op jit(solution)/shard_map/reshape | solution.py:332
  2.7 0.7 %reshape.40.value_bias_ref = f32[1,384]{1,0:T(1,128)S(1)} reshape(f32[384]{0:T(512)} %param.25) | data formatting | bytes 3072 | tf_op jit(solution)/shard_map/reshape | solution.py:332
  3.4 0.7 %reshape.41.out_bias_ref = f32[1,384]{1,0:T(1,128)S(1)} reshape(f32[384]{0:T(512)} %param.27) | data formatting | bytes 3072 | tf_op jit(solution)/shard_map/reshape | solution.py:332
  4.1 0.0 copy-start
  4.1 1.0 %copy-done = bf16[384,384]{1,0:T(8,128)(2,1)S(1)} copy-done((bf16[384,384]{1,0:T(8,128)(2,1)S(1)}, bf16[384,384]{1,0:T(8,128)(2,1)}, u32[]{:S(2)}) %copy-start) | copy-done | bytes 294936
  5.1 0.0 copy-start.1
  5.1 1.0 %copy-done.1 = bf16[384,384]{1,0:T(8,128)(2,1)S(1)} copy-done((bf16[384,384]{1,0:T(8,128)(2,1)S(1)}, bf16[384,384]{1,0:T(8,128)(2,1)}, u32[]{:S(2)}) %copy-start.1) | copy-done | bytes 294936
  6.0 0.0 copy-start.2
  6.0 1.0 %copy-done.2 = bf16[384,384]{1,0:T(8,128)(2,1)S(1)} copy-done((bf16[384,384]{1,0:T(8,128)(2,1)S(1)}, bf16[384,384]{1,0:T(8,128)(2,1)}, u32[]{:S(2)}) %copy-start.2) | copy-done | bytes 294936
  7.0 0.0 copy-start.3
  7.0 1.0 %copy-done.3 = bf16[384,384]{1,0:T(8,128)(2,1)S(1)} copy-done((bf16[384,384]{1,0:T(8,128)(2,1)S(1)}, bf16[384,384]{1,0:T(8,128)(2,1)}, u32[]{:S(2)}) %copy-start.3) | copy-done | bytes 294936
  7.9 0.0 copy-start.4
  8.0 0.9 %copy-done.4 = bf16[1,2,4,32,384]{4,3,2,1,0:T(8,128)(2,1)S(1)} copy-done((bf16[1,2,4,32,384]{4,3,2,1,0:T(8,128)(2,1)S(1)}, bf16[1,2,4,32,384]{4,3,2,1,0:T(8,128)(2,1)}, u32[]{:S(2)}) %copy-start.4) | copy-done | bytes 196632
  8.9 0.0 copy-start.5
  8.9 0.9 %copy-done.5 = bf16[1,4,32,384]{3,2,1,0:T(8,128)(2,1)S(1)} copy-done((bf16[1,4,32,384]{3,2,1,0:T(8,128)(2,1)S(1)}, bf16[1,4,32,384]{3,2,1,0:T(8,128)(2,1)}, u32[]{:S(2)}) %copy-start.5) | copy-done | bytes 98328
  9.8 0.0 copy-start.6
  9.8 0.9 %copy-done.6 = bf16[1,4,32,384]{3,2,1,0:T(8,128)(2,1)S(1)} copy-done((bf16[1,4,32,384]{3,2,1,0:T(8,128)(2,1)S(1)}, bf16[1,4,32,384]{3,2,1,0:T(8,128)(2,1)}, u32[]{:S(2)}) %copy-start.6) | copy-done | bytes 98328
  10.7 30.1 %shard_map.136 = bf16[128,384]{1,0:T(8,128)(2,1)S(1)} custom-call(bf16[128,384]{1,0:T(8,128)(2,1)S(1)} %bitcast.7, bf16[2,128,384]{2,1,0:T(8,128)(2,1)S(1)} %bitcast.6, bf16[128,384]{1,0:T(8,128)(2,1)S(1)} %bitcast.8, f32[1,384]{1,0:T(1,128)S(1)} %reshape.36.gain_one_ref, f32[1,384]{1,0:T(1,128)S(1)} %reshape.37.conv_bias_ref, ...), custom_call_target="tpu_custom_call" | custom-call | flops 1610612736 | bytes 10027008 | tf_op jit(solution)/shard_map/pallas_call | solution.py:337
  40.8 0.6 %copy.16 = bf16[1,4,32,384]{3,2,1,0:T(8,128)(2,1)} copy(bf16[1,4,32,384]{3,2,1,0:T(8,128)(2,1)S(1)} %bitcast.5) | data formatting | bytes 196608
Async XLA Ops:
  4.1 1.0 %copy-start = (bf16[384,384]{1,0:T(8,128)(2,1)S(1)}, bf16[384,384]{1,0:T(8,128)(2,1)}, u32[]{:S(2)}) copy-start(bf16[384,384]{1,0:T(8,128)(2,1)} %query_hbm.1) | copy-start | bytes 884740
  5.1 1.0 %copy-start.1 = (bf16[384,384]{1,0:T(8,128)(2,1)S(1)}, bf16[384,384]{1,0:T(8,128)(2,1)}, u32[]{:S(2)}) copy-start(bf16[384,384]{1,0:T(8,128)(2,1)} %key_hbm.1) | copy-start | bytes 884740
  6.0 1.0 %copy-start.2 = (bf16[384,384]{1,0:T(8,128)(2,1)S(1)}, bf16[384,384]{1,0:T(8,128)(2,1)}, u32[]{:S(2)}) copy-start(bf16[384,384]{1,0:T(8,128)(2,1)} %value_hbm.1) | copy-start | bytes 884740
  7.0 1.0 %copy-start.3 = (bf16[384,384]{1,0:T(8,128)(2,1)S(1)}, bf16[384,384]{1,0:T(8,128)(2,1)}, u32[]{:S(2)}) copy-start(bf16[384,384]{1,0:T(8,128)(2,1)} %out_hbm.1) | copy-start | bytes 884740
  7.9 0.9 %copy-start.4 = (bf16[1,2,4,32,384]{4,3,2,1,0:T(8,128)(2,1)S(1)}, bf16[1,2,4,32,384]{4,3,2,1,0:T(8,128)(2,1)}, u32[]{:S(2)}) copy-start(bf16[1,2,4,32,384]{4,3,2,1,0:T(8,128)(2,1)} %param.15) | copy-start | bytes 589828
  8.9 0.9 %copy-start.5 = (bf16[1,4,32,384]{3,2,1,0:T(8,128)(2,1)S(1)}, bf16[1,4,32,384]{3,2,1,0:T(8,128)(2,1)}, u32[]{:S(2)}) copy-start(bf16[1,4,32,384]{3,2,1,0:T(8,128)(2,1)} %param.14) | copy-start | bytes 294916
  9.8 0.9 %copy-start.6 = (bf16[1,4,32,384]{3,2,1,0:T(8,128)(2,1)S(1)}, bf16[1,4,32,384]{3,2,1,0:T(8,128)(2,1)}, u32[]{:S(2)}) copy-start(bf16[1,4,32,384]{3,2,1,0:T(8,128)(2,1)} %param.16) | copy-start | bytes 294916

commit v2 on v1

--- a/solution.py
+++ b/solution.py
@@ -21,12 +21,14 @@
 
 def kernel(
     R, K, cores, TR, TC, C, E,
+    hidden_hbm, cache_hbm, shortcut_hbm, gain_one_hbm, conv_bias_hbm, gain_two_hbm,
+    query_bias_hbm, value_bias_hbm, out_bias_hbm,
+    conv_hbm, query_hbm, key_hbm, value_hbm, out_hbm,
+    o_ref,
     hidden_ref, cache_ref, shortcut_ref, gain_one_ref, conv_bias_ref, gain_two_ref,
     query_bias_ref, value_bias_ref, out_bias_ref,
-    conv_hbm, query_hbm, key_hbm, value_hbm, out_hbm,
-    o_ref,
     conv_w, proj_w, xs, sr, sc, hr, hc, edge, G, run_max, run_sum, acc,
-    conv_sem, proj_sem, hsend, hrecv, zsem, xsem, csem, rsem,
+    in_sem, conv_sem, proj_sem, hsend, hrecv, zsem, xsem, csem, rsem,
 ):
     X = K // cores
     N = TR * TC
@@ -34,6 +36,25 @@
     col = lax.axis_index("cols")
     x = col // cores
     c = col % cores
+
+    in_copies = [
+        pltpu.make_async_copy(source, target, in_sem.at[k])
+        for k, (source, target) in enumerate(
+            (
+                (hidden_hbm, hidden_ref),
+                (gain_one_hbm, gain_one_ref),
+                (cache_hbm, cache_ref),
+                (shortcut_hbm, shortcut_ref),
+                (conv_bias_hbm, conv_bias_ref),
+                (gain_two_hbm, gain_two_ref),
+                (query_bias_hbm, query_bias_ref),
+                (value_bias_hbm, value_bias_ref),
+                (out_bias_hbm, out_bias_ref),
+            )
+        )
+    ]
+    for copy in in_copies:
+        copy.start()
 
     has_up = r > 0
     has_down = r < R - 1
@@ -77,6 +98,8 @@
     for copy in conv_copies + proj_copies:
         copy.start()
 
+    for copy in in_copies[:3]:
+        copy.wait()
     current = normalize(hidden_ref[...].astype(f32), gain_one_ref[...])
     activated = (current / (1.0 + jnp.exp(-current))).astype(bf16)
     position = lax.broadcasted_iota(jnp.int32, (16, 1), 0)
@@ -157,6 +180,8 @@
                 position == 15, sides[1][v][k : k + 1], xs[f, last, 2 * C : 3 * C].astype(f32)
             ).astype(bf16)
 
+    for copy in in_copies[3:]:
+        copy.wait()
     total = jnp.zeros((N, C), f32)
     for f in range(3):
         for a in range(3):
@@ -217,7 +242,7 @@
                 core_move(origin, xp).start()
 
     def at_distance(s, action):
-        @pl.when(r - s >= 0)
+        @pl.when(jnp.logical_and(s >= 0, r - s >= 0))
         def _():
             action(r - s)
 
@@ -265,6 +290,7 @@
 
         at_distance(s, receive)
         at_distance(s - 1, relay)
+        at_distance(s - 2, attend)
         return carry
 
     lax.fori_loop(1, R, step, 0)
@@ -274,7 +300,7 @@
         at_distance(s, attend)
         return carry
 
-    lax.fori_loop(0, R, attend_step, 0)
+    lax.fori_loop(max(R - 2, 0), R, attend_step, 0)
 
     context = (acc[...] / run_sum[...]).astype(bf16)
     attended = (
@@ -329,7 +355,6 @@
     cores = 2 if K % 2 == 0 else 1
     X = K // cores
     E = -(-3 * TR // 16) * 16
-    vector = lambda v: v.reshape(1, C)
     vmem = pl.BlockSpec(memory_space=pltpu.VMEM)
     hbm = pl.BlockSpec(memory_space=pltpu.HBM)
     dma = pltpu.SemaphoreType.DMA
@@ -337,9 +362,15 @@
     decoded = pl.pallas_call(
         functools.partial(kernel, R, K, cores, TR, TC, C, E),
         out_shape=jax.ShapeDtypeStruct((N, C), bf16),
-        in_specs=[vmem] * 9 + [hbm] * 5,
+        in_specs=[hbm] * 14,
         out_specs=vmem,
         scratch_shapes=[
+            pltpu.VMEM((N, C), bf16),
+            pltpu.VMEM((2, N, C), bf16),
+            pltpu.VMEM((N, C), bf16),
+        ]
+        + [pltpu.VMEM((C,), f32)] * 6
+        + [
             pltpu.VMEM((9, 3 * C, C), bf16),
             pltpu.VMEM((4, C, C), bf16),
             pltpu.VMEM((3, N + 2 * TC, 3 * C), bf16),
@@ -353,6 +384,7 @@
             pltpu.VMEM((N, 1), f32),
             pltpu.VMEM((N, C), f32),
             dma((9,)),
+            dma((9,)),
             dma((4,)),
             dma((8,)),
             dma((8,)),
@@ -362,7 +394,7 @@
             dma((R, K)),
         ],
         compiler_params=pltpu.CompilerParams(
-            collective_id=0, has_side_effects=True, vmem_limit_bytes=48 * 1024 * 1024
+            collective_id=0, has_side_effects=True, vmem_limit_bytes=63 * 1024 * 1024
         ),
         cost_estimate=pl.CostEstimate(
             flops=flops, bytes_accessed=2 * C * (32 * C + 6 * N), transcendentals=R * K * N * N
@@ -371,12 +403,12 @@
         hidden.reshape(N, C),
         frame_cache.reshape(2, N, C),
         shortcut.reshape(N, C),
-        vector(gain_one),
-        vector(conv_bias),
-        vector(gain_two),
-        vector(query_bias),
-        vector(value_bias),
-        vector(out_bias),
+        gain_one,
+        conv_bias,
+        gain_two,
+        query_bias,
+        value_bias,
+        out_bias,
         conv_weight.reshape(9, 3 * C, C),
         query_weight,
         key_weight,

time: 41.9 us -> 31.5 us (0.75)
  local copies, waits for them, and re-layouts: 11.3 us -> 1.54 us
  Pallas kernels: 30.1 us -> 29.6 us
    unnamed x15 -> x1, local copies, waits for them, and re-layouts: 7.2 us -> 1.54 us
    reshape x6 -> x0, local copies, waits for them, and re-layouts: 4.1 us -> none  [per_device(): vector = lambda v: v.reshape(1, C)]
    pallas_call x1, Pallas kernels: 30.1 us -> 29.6 us  [per_device(): pl.pallas_call(functools.partial(kernel, R, K, cores, TR, TC, C, E), out_...]
where the time goes in v2:
time: 31.5 us; the launch traced here: 31.1 us
  Pallas kernels  29.6 us (94%)
  local copies, waits for them, and re-layouts  1.54 us (5%)
    pallas_call x1, Pallas kernels, per_device(): pl.pallas_call(functools.partial(kernel, R, K, cores, TR, TC, C, E), out_...  29.6 us
    unnamed x1, local copies, waits for them, and re-layouts  1.54 us

profile of v2, /device:TPU:0, one launch (start us, length us, event | category | flops | bytes accessed | tf_op | source)
XLA Modules:
  0.0 31.1 jit_solution(14984277718091303152)
XLA Ops:
  0.0 29.6 %shard_map.136 = bf16[128,384]{1,0:T(8,128)(2,1)} custom-call(bf16[128,384]{1,0:T(8,128)(2,1)} %bitcast.8, bf16[2,128,384]{2,1,0:T(8,128)(2,1)} %bitcast.7, bf16[128,384]{1,0:T(8,128)(2,1)} %bitcast.9, f32[384]{0:T(512)} %gain_one_hbm.1, f32[384]{0:T(512)} %conv_bias_hbm.1, f32[384]{0:T(512)} %gain_two_hbm.1, f32[384]{0:T(512)} %query_bias_hbm.1, ...), custom_call_target="tpu_custom_call" | custom-call | flops 1610612736 | bytes 10027008 | tf_op jit(solution)/shard_map/pallas_call | solution.py:362
  29.6 1.5 %copy.16 = bf16[1,4,32,384]{3,2,1,0:T(8,128)(2,1)} copy(bf16[1,4,32,384]{3,2,1,0:T(8,128)(2,1)} %bitcast.6) | data formatting | bytes 196608

commit v3 on v2

--- a/solution.py
+++ b/solution.py
@@ -9,6 +9,7 @@
 from jax.sharding import PartitionSpec as P
 
 norm_epsilon = 1e-06
+pieces = 2
 f32 = jnp.float32
 bf16 = jnp.bfloat16
 MESH = pl.DeviceIdType.MESH
@@ -32,6 +33,7 @@
 ):
     X = K // cores
     N = TR * TC
+    M = N // pieces
     r = lax.axis_index("rows")
     col = lax.axis_index("cols")
     x = col // cores
@@ -112,9 +114,6 @@
             k = f * TR + i
             edge[0, k : k + 1] = wide[i * TC : i * TC + 1]
             edge[1, k : k + 1] = wide[(i + 1) * TC - 1 : (i + 1) * TC]
-        xs[f, TC : TC + N, C : 2 * C] = frame
-        xs[f, TC : TC + N, 0:C] = pltpu.roll(wide, 1, 0).astype(bf16)
-        xs[f, TC : TC + N, 2 * C : 3 * C] = pltpu.roll(wide, N - 1, 0).astype(bf16)
     if E > 3 * TR:
         for side in range(2):
             edge[side, 3 * TR : E] = jnp.zeros((E - 3 * TR, C), f32)
@@ -141,6 +140,13 @@
         @pl.when(exists(dr, dc))
         def _():
             halo(dr, dc).start()
+
+    for f in range(3):
+        frame = activated if f == 2 else cache_ref[f]
+        wide = frame.astype(f32)
+        xs[f, TC : TC + N, C : 2 * C] = frame
+        xs[f, TC : TC + N, 0:C] = pltpu.roll(wide, 1, 0).astype(bf16)
+        xs[f, TC : TC + N, 2 * C : 3 * C] = pltpu.roll(wide, N - 1, 0).astype(bf16)
 
     for dr, dc in neighbours:
         ok = exists(dr, dc)
@@ -198,21 +204,22 @@
 
     G[r, span(col)] = normed
 
-    def move(origin, which, send, row_to, col_to):
-        block = G.at[origin, span(which)]
+    def move(origin, which, piece, send, row_to, col_to):
+        start = pl.multiple_of(which * N + piece * M, M)
+        block = G.at[origin, pl.ds(start, M)]
         return pltpu.make_async_remote_copy(
-            src_ref=block, dst_ref=block, send_sem=send, recv_sem=rsem.at[origin, which],
+            src_ref=block, dst_ref=block, send_sem=send, recv_sem=rsem.at[origin, which, piece],
             device_id={"rows": row_to, "cols": col_to}, device_id_type=MESH,
         )
 
-    def z_move(origin, way):
-        return move(origin, col, zsem.at[origin, way], r + (1 if way else -1), col)
-
-    def x_move(origin, d):
-        return move(origin, col, xsem.at[origin, d], r, x_peers[d] * cores + c)
-
-    def core_move(origin, xp):
-        return move(origin, xp * cores + c, csem.at[origin, xp], r, x * cores + 1 - c)
+    def z_move(origin, way, h):
+        return move(origin, col, h, zsem.at[origin, way, h], r + (1 if way else -1), col)
+
+    def x_move(origin, d, h):
+        return move(origin, col, h, xsem.at[origin, d, h], r, x_peers[d] * cores + c)
+
+    def core_move(origin, xp, h):
+        return move(origin, xp * cores + c, h, csem.at[origin, xp, h], r, x * cores + 1 - c)
 
     def z_conditions(origin):
         return (
@@ -220,26 +227,27 @@
             jnp.logical_and(origin <= r, has_down),
         )
 
-    def spread(origin):
+    def spread(origin, h):
         for way, ok in enumerate(z_conditions(origin)):
 
             @pl.when(ok)
             def _():
-                z_move(origin, way).start()
+                z_move(origin, way, h).start()
 
         for d in range(X - 1):
-            x_move(origin, d).start()
+            x_move(origin, d, h).start()
         if cores == 2:
-            core_move(origin, x).start()
-
-    def arrived(origin, which):
-        move(origin, which, zsem.at[origin, 0], r, col).wait_recv()
+            core_move(origin, x, h).start()
+
+    def arrived(origin, which, h):
+        move(origin, which, h, zsem.at[origin, 0, h], r, col).wait_recv()
 
     def relay(origin):
-        for xp in x_peers:
-            arrived(origin, xp * cores + c)
-            if cores == 2:
-                core_move(origin, xp).start()
+        for h in range(pieces):
+            for xp in x_peers:
+                arrived(origin, xp * cores + c, h)
+                if cores == 2:
+                    core_move(origin, xp, h).start()
 
     def at_distance(s, action):
         @pl.when(jnp.logical_and(s >= 0, r - s >= 0))
@@ -250,7 +258,8 @@
         def _():
             action(r + s)
 
-    spread(r)
+    for h in range(pieces):
+        spread(r, h)
 
     for copy in proj_copies:
         copy.wait()
@@ -270,7 +279,8 @@
     def attend(origin):
         if cores == 2:
             for xp in range(X):
-                arrived(origin, xp * cores + 1 - c)
+                for h in range(pieces):
+                    arrived(origin, xp * cores + 1 - c, h)
         piece = G[origin]
         scores = lax.dot_general(folded, piece, contract_last, preferred_element_type=f32)
         old_max = run_max[...]
@@ -284,11 +294,13 @@
         )
 
     def step(s, carry):
-        def receive(origin):
-            arrived(origin, col)
-            spread(origin)
-
-        at_distance(s, receive)
+        for h in range(pieces):
+
+            def receive(origin):
+                arrived(origin, col, h)
+                spread(origin, h)
+
+            at_distance(s, receive)
         at_distance(s - 1, relay)
         at_distance(s - 2, attend)
         return carry
@@ -316,17 +328,18 @@
             halo(dr, dc).wait_send()
 
     def drain(origin, carry):
-        for way, ok in enumerate(z_conditions(origin)):
-
-            @pl.when(ok)
-            def _():
-                z_move(origin, way).wait_send()
-
-        for d in range(X - 1):
-            x_move(origin, d).wait_send()
-        if cores == 2:
-            for xp in range(X):
-                core_move(origin, xp).wait_send()
+        for h in range(pieces):
+            for way, ok in enumerate(z_conditions(origin)):
+
+                @pl.when(ok)
+                def _():
+                    z_move(origin, way, h).wait_send()
+
+            for d in range(X - 1):
+                x_move(origin, d, h).wait_send()
+            if cores == 2:
+                for xp in range(X):
+                    core_move(origin, xp, h).wait_send()
         return carry
 
     lax.fori_loop(0, R, drain, 0)
@@ -388,18 +401,19 @@
             dma((4,)),
             dma((8,)),
             dma((8,)),
-            dma((R, 2)),
-            dma((R, max(X - 1, 1))),
-            dma((R, X)),
-            dma((R, K)),
+            dma((R, 2, pieces)),
+            dma((R, max(X - 1, 1), pieces)),
+            dma((R, X, pieces)),
+            dma((R, K, pieces)),
         ],
         compiler_params=pltpu.CompilerParams(
-            collective_id=0, has_side_effects=True, vmem_limit_bytes=63 * 1024 * 1024
+            collective_id=0, has_side_effects=True, vmem_limit_bytes=48 * 1024 * 1024
         ),
         cost_estimate=pl.CostEstimate(
             flops=flops, bytes_accessed=2 * C * (32 * C + 6 * N), transcendentals=R * K * N * N
         ),
-    )(
+    )
+    operands = (
         hidden.reshape(N, C),
         frame_cache.reshape(2, N, C),
         shortcut.reshape(N, C),
@@ -415,6 +429,7 @@
         value_weight,
         out_weight,
     )
+    decoded = decoded(*[pltpu.with_memory_space_constraint(v, pltpu.HBM) for v in operands])
     return decoded.reshape(1, TR, TC, C)
 
 

time: 31.5 us -> 29.2 us (0.927)
  Pallas kernels: 29.6 us -> 28.3 us
  local copies, waits for them, and re-layouts: 1.54 us -> 0.64 us
    pallas_call x1, Pallas kernels: 29.6 us -> 28.3 us  [per_device(): decoded(*[pltpu.with_memory_space_constraint(v, pltpu.HBM) for v in opera...]
    unnamed x1, local copies, waits for them, and re-layouts: 1.54 us -> 0.64 us
where the time goes in v3:
time: 29.2 us; the launch traced here: 28.9 us
  Pallas kernels  28.3 us (97%)
  local copies, waits for them, and re-layouts  0.64 us (2%)
    pallas_call x1, Pallas kernels, per_device(): decoded(*[pltpu.with_memory_space_constraint(v, pltpu.HBM) for v in opera...  28.3 us
    unnamed x1, local copies, waits for them, and re-layouts  0.64 us

profile of v3, /device:TPU:0, one launch (start us, length us, event | category | flops | bytes accessed | tf_op | source)
XLA Modules:
  0.0 28.9 jit_solution(17390742779298892494)
XLA Ops:
  0.0 28.3 %shard_map.136 = bf16[128,384]{1,0:T(8,128)(2,1)S(1)} custom-call(bf16[128,384]{1,0:T(8,128)(2,1)} %bitcast.8, bf16[2,128,384]{2,1,0:T(8,128)(2,1)} %bitcast.7, bf16[128,384]{1,0:T(8,128)(2,1)} %bitcast.9, f32[384]{0:T(512)} %gain_one_hbm.1, f32[384]{0:T(512)} %conv_bias_hbm.1, f32[384]{0:T(512)} %gain_two_hbm.1, f32[384]{0:T(512)} %query_bias_hbm.1, ...), custom_call_target="tpu_custom_call" | custom-call | flops 1610612736 | bytes 10027008 | tf_op jit(solution)/shard_map/pallas_call | solution.py:432
  28.3 0.6 %copy.16 = bf16[1,4,32,384]{3,2,1,0:T(8,128)(2,1)} copy(bf16[1,4,32,384]{3,2,1,0:T(8,128)(2,1)S(1)} %bitcast.5) | data formatting | bytes 196608
